TPU v7x, 32 devices: a whole 2x2x4 slice. The times are simulated.
32 devices in a mesh: group: 2 (over x), example: 16 (over z, y, core).
Axes of the slice: x: 2, y: 2, z: 4, core: 2. Of those that a mesh axis runs over, the one named last changes fastest.
Arguments:
- train_grads: bfloat16 [32768, 4096], P(('group', 'example')), parts along dimension 0, may hold values from -6 to 6
- query_grads: bfloat16 [6144, 4096], P(('group', 'example')), parts along dimension 0, may hold values from -6 to 6
- left_inverse: bfloat16 [2, 64, 64], P('group'), parts along dimension 0, may hold values from -0.75 to 0.75
- right_inverse: bfloat16 [2, 64, 64], P('group'), parts along dimension 0, may hold values from -0.75 to 0.75
Outputs:
- scores: float32 [32768, 768], P(('group', 'example')), parts along dimension 0
- query_mass: float32 [6144, 1], P(('group', 'example')), parts along dimension 0
There are 2 independent parts, one for each index of `group`. A program takes and returns all parts, laid end to end along the dimension named above; each array names one. Nothing has to cross between parts.
All inputs are finite; a program needn't handle non-finite values.
Results may differ from a plain program's by a relative error of at most 0.0041.
Values may be sent and summed in bfloat16 or wider, within the bound.
A program may use at most 64 MiB of HBM per device.

v0:
```python
import jax
import jax.numpy as jnp
from jax import lax
from jax.sharding import PartitionSpec as P

SHIFTS = 3


def from_behind(value, axis, steps):
    count = lax.axis_size(axis)
    pairs = [(source, (source + steps) % count) for source in range(count)]
    return lax.ppermute(value, axis, pairs)


def precondition(query_grads, left_inverse, right_inverse):
    count = query_grads.shape[0]
    modules = left_inverse.shape[0]
    side = left_inverse.shape[1]
    mats = query_grads.reshape(count, modules, side, side)
    inner = jnp.einsum(
        "mab,qmbc->qmac", left_inverse, mats, preferred_element_type=jnp.float32
    ).astype(jnp.bfloat16)
    outer = jnp.einsum("qmac,mcd->qmad", inner, right_inverse, preferred_element_type=jnp.float32)
    return outer.reshape(count, modules * side * side).astype(jnp.bfloat16)


def score_block(train_grads, block, mdim):
    scale = 1.0 / jnp.sqrt(jnp.float32(mdim))
    part = (
        lax.dot_general(
            train_grads, block, (((1,), (1,)), ((), ())), preferred_element_type=jnp.float32
        )
        * scale
    )
    module_mass = [jnp.sum(part * part, axis=0)]
    return (part, jnp.stack(module_mass, axis=1))


def local(train_grads, query_grads, left_inverse, right_inverse):
    mdim = left_inverse.shape[1] * left_inverse.shape[2]
    rows = train_grads.shape[0]
    precond = precondition(query_grads, left_inverse, right_inverse)
    block = precond
    columns = []
    partials = []
    for step_num in range(SHIFTS + 1):
        if step_num > 0:
            block = from_behind(block, "example", 1)
        total, module_mass = score_block(train_grads, block, mdim)
        columns.append(total)
        partials.append(module_mass)
    scores = jnp.concatenate(columns, axis=1)
    denom = jnp.float32((SHIFTS + 1) * rows)
    summed = partials[0]
    for step_num in range(1, SHIFTS + 1):
        summed = summed + from_behind(partials[step_num], "example", -step_num)
    return (scores, summed / denom)


def solution(mesh):
    return jax.shard_map(
        local,
        mesh=mesh,
        in_specs=(
            P(("group", "example"), None),
            P(("group", "example"), None),
            P("group", None, None),
            P("group", None, None),
        ),
        out_specs=(P(("group", "example"), None), P(("group", "example"), None)),
        check_vma=False,
    )
```

profile of v0, /device:TPU:0, one launch (start us, length us, event | category | flops | bytes accessed | tf_op | source)
XLA Modules:
  0.0 86.9 jit_solution(7132129020563786623)
XLA Ops:
  0.6 0.0 copy-start
  0.6 3.2 %copy.15 = bf16[192,4096]{0,1:T(8,128)(2,1)S(1)} copy(bf16[192,4096]{1,0:T(8,128)(2,1)} %param.5) | data formatting | bytes 3145728 | tf_op args[1]
  3.8 0.0 copy-start.1
  3.8 1.7 %convert_bitcast_fusion = bf16[192,64,64]{0,1,2:T(8,128)(2,1)S(1)} fusion(bf16[192,64,64]{0,2,1:T(8,128)(2,1)S(1)} %bitcast.45, bf16[1,64,64]{2,1,0:T(8,128)(2,1)S(1)} %copy-done), kind=kOutput, calls=%fused_computation.5 | convolution fusion | flops 101449728 | bytes 3153920 | tf_op jit(solution)/shard_map/mab,qmbc->qmac/dot_general | solution.py:20
  5.6 1.7 %fusion.6 = bf16[192,64,64]{0,2,1:T(8,128)(2,1)S(1)} fusion(bf16[192,64,64]{0,1,2:T(8,128)(2,1)S(1)} %convert_bitcast_fusion, bf16[1,64,64]{2,1,0:T(8,128)(2,1)S(1)} %copy-done.1), kind=kOutput, calls=%fused_computation.6 | convolution fusion | flops 101449728 | bytes 3153920 | tf_op jit(solution)/shard_map/qmac,mcd->qmad/dot_general | solution.py:23
  7.3 2.7 %copy.19 = bf16[192,4096]{1,0:T(8,128)(2,1)} copy(bf16[192,4096]{0,1:T(8,128)(2,1)S(1)} %bitcast.43) | data formatting | bytes 3145728 | tf_op jit(solution)/shard_map/convert_element_type | solution.py:24
  10.0 0.5 collective-permute-start
  10.5 23.3 %collective-permute-done = bf16[192,4096]{1,0:T(8,128)(2,1)S(1)} collective-permute-done((bf16[192,4096]{1,0:T(8,128)(2,1)}, bf16[192,4096]{1,0:T(8,128)(2,1)S(1)}, u32[]{:S(2)}, u32[]{:S(2)}) %collective-permute-start) | collective-permute-done | bytes 1572896 | tf_op jit(solution)/shard_map/ppermute | solution.py:12
  33.8 22.5 %collective-permute-done.1 = bf16[192,4096]{1,0:T(8,128)(2,1)S(1)} collective-permute-done((bf16[192,4096]{1,0:T(8,128)(2,1)S(1)}, bf16[192,4096]{1,0:T(8,128)(2,1)S(1)}, u32[]{:S(2)}, u32[]{:S(2)}) %collective-permute-start.1) | collective-permute-done | bytes 1572896 | tf_op jit(solution)/shard_map/ppermute | solution.py:12
  56.3 0.0 collective-permute-start.2
  56.3 6.3 %multiply_reduce_fusion.3 = (f32[192]{0:T(256)S(1)}, f32[1024,192]{0,1:T(8,128)S(1)}) fusion(bf16[192,4096]{0,1:T(8,128)(2,1)S(1)} %bitcast.44, bf16[1024,4096]{1,0:T(8,128)(2,1)} %param.4), kind=kOutput, calls=%fused_computation.18 | convolution fusion | flops 1611202304 | bytes 10748672 | tf_op jit(solution)/shard_map/dot_general | solution.py:30
  62.6 0.0 slice-start
  62.6 6.5 %multiply_reduce_fusion.2 = (f32[192]{0:T(256)S(1)}, f32[1024,192]{0,1:T(8,128)S(1)}) fusion(bf16[192,4096]{1,0:T(8,128)(2,1)S(1)} %collective-permute-done, bf16[1024,4096]{1,0:T(8,128)(2,1)} %param.4), kind=kOutput, calls=%fused_computation.17 | convolution fusion | flops 1611202304 | bytes 10748672 | tf_op jit(solution)/shard_map/dot_general | solution.py:30
  69.2 0.0 slice-start.1
  69.2 4.5 %collective-permute-start.3 = (f32[192,1]{0,1:T(1,128)S(1)}, f32[192,1]{0,1:T(1,128)S(1)}, u32[]{:S(2)}, u32[]{:S(2)}) collective-permute-start(f32[192,1]{0,1:T(1,128)S(1)} %bitcast.49), channel_id=1, source_target_pairs={{0,15},{1,0},{2,1},{3,2},{4,3},{5,4},{6,5},{7,6},{8,7},{9,8},{10,9... | collective-permute-start | bytes 2312 | tf_op jit(solution)/shard_map/ppermute | solution.py:12
  73.7 6.4 %multiply_reduce_fusion.1 = (f32[192]{0:T(256)S(1)}, f32[1024,192]{0,1:T(8,128)S(1)}) fusion(bf16[192,4096]{1,0:T(8,128)(2,1)S(1)} %collective-permute-done.1, bf16[1024,4096]{1,0:T(8,128)(2,1)} %param.4), kind=kOutput, calls=%fused_computation.16 | convolution fusion | flops 1611202304 | bytes 10748672 | tf_op jit(solution)/shard_map/dot_general | solution.py:30
  80.0 0.2 collective-permute-start.4
  80.3 0.0 collective-permute-done.2
  80.3 3.0 %multiply_reduce_fusion = (f32[192]{0:T(256)S(1)}, f32[1024,192]{0,1:T(8,128)S(1)}) fusion(bf16[192,4096]{1,0:T(8,128)(2,1)S(1)} %collective-permute-done.2, bf16[1024,4096]{1,0:T(8,128)(2,1)S(1)} %bitcast.48), kind=kOutput, calls=%fused_computation.15 | convolution fusion | flops 1611202304 | bytes 10748672 | tf_op jit(solution)/shard_map/dot_general | solution.py:30
  83.3 0.1 collective-permute-start.5
  83.4 0.4 pad_maximum_fusion
  83.7 2.4 %copy.20 = f32[1024,768]{1,0:T(8,128)} copy(f32[1024,768]{0,1:T(8,128)S(1)} %pad_maximum_fusion) | data formatting | bytes 6291456
  86.1 0.2 collective-permute-done.5
  86.4 0.6 add_multiply_fusion
  (8 shorter events, 0.0 us)
Async XLA Ops:
  0.6 3.2 %copy-start = (bf16[1,64,64]{2,1,0:T(8,128)(2,1)S(1)}, bf16[1,64,64]{2,1,0:T(8,128)(2,1)}, u32[]{:S(2)}) copy-start(bf16[1,64,64]{2,1,0:T(8,128)(2,1)} %param.6) | copy-start | bytes 24580
  3.8 1.7 %copy-start.1 = (bf16[1,64,64]{2,1,0:T(8,128)(2,1)S(1)}, bf16[1,64,64]{2,1,0:T(8,128)(2,1)}, u32[]{:S(2)}) copy-start(bf16[1,64,64]{2,1,0:T(8,128)(2,1)} %param.7) | copy-start | bytes 24580
  10.0 23.7 %collective-permute-start = (bf16[192,4096]{1,0:T(8,128)(2,1)}, bf16[192,4096]{1,0:T(8,128)(2,1)S(1)}, u32[]{:S(2)}, u32[]{:S(2)}) collective-permute-start(bf16[192,4096]{1,0:T(8,128)(2,1)} %copy.19), channel_id=1, source_target_pairs={{0,1},{1,2},{2,3},{3,4},{4,5},{5,6},{6,7},{7,8},{8,9},{9,10},{10,1... | collective-permute-start | bytes 4718600 | tf_op jit(solution)/shard_map/ppermute | solution.py:12
  33.8 22.5 %collective-permute-start.1 = (bf16[192,4096]{1,0:T(8,128)(2,1)S(1)}, bf16[192,4096]{1,0:T(8,128)(2,1)S(1)}, u32[]{:S(2)}, u32[]{:S(2)}) collective-permute-start(bf16[192,4096]{1,0:T(8,128)(2,1)S(1)} %collective-permute-done), channel_id=1, source_target_pairs={{0,1},{1,2},{2,3},{3,4},{4,5},{5,6},{6,7},{7,8},{8,9},{9,10},{10,1... | collective-permute-start | bytes 4718600 | tf_op jit(solution)/shard_map/ppermute | solution.py:12
  56.3 24.0 %collective-permute-start.2 = (bf16[192,4096]{1,0:T(8,128)(2,1)S(1)}, bf16[192,4096]{1,0:T(8,128)(2,1)S(1)}, u32[]{:S(2)}, u32[]{:S(2)}) collective-permute-start(bf16[192,4096]{1,0:T(8,128)(2,1)S(1)} %collective-permute-done.1), channel_id=1, source_target_pairs={{0,1},{1,2},{2,3},{3,4},{4,5},{5,6},{6,7},{7,8},{8,9},{9,10},{10,1... | collective-permute-start | bytes 4718600 | tf_op jit(solution)/shard_map/ppermute | solution.py:12
  62.6 17.7 %slice-start = ((s8[8388608]{0:T(1024)(128)(4,1)}), s8[4194304]{0:T(1024)(128)(4,1)S(1)}, s32[]{:S(2)}) async-start(s8[8388608]{0:T(1024)(128)(4,1)} %bitcast.47), calls=%async_computation | async-start | bytes 8388608
  69.2 11.1 %slice-start.1 = ((s8[8388608]{0:T(1024)(128)(4,1)}), s8[4194304]{0:T(1024)(128)(4,1)S(1)}, s32[]{:S(2)}) async-start(s8[8388608]{0:T(1024)(128)(4,1)} %bitcast.47), calls=%async_computation.1 | async-start | bytes 8388608
  69.2 16.9 %collective-permute-start.3 = (f32[192,1]{0,1:T(1,128)S(1)}, f32[192,1]{0,1:T(1,128)S(1)}, u32[]{:S(2)}, u32[]{:S(2)}) collective-permute-start(f32[192,1]{0,1:T(1,128)S(1)} %bitcast.49), channel_id=1, source_target_pairs={{0,15},{1,0},{2,1},{3,2},{4,3},{5,4},{6,5},{7,6},{8,7},{9,8},{10,9... | collective-permute-start | bytes 2312 | tf_op jit(solution)/shard_map/ppermute | solution.py:12
  80.0 6.1 %collective-permute-start.4 = (f32[192,1]{0,1:T(1,128)S(1)}, f32[192,1]{0,1:T(1,128)S(1)}, u32[]{:S(2)}, u32[]{:S(2)}) collective-permute-start(f32[192,1]{0,1:T(1,128)S(1)} %bitcast.50), channel_id=1, source_target_pairs={{0,14},{1,15},{2,0},{3,1},{4,2},{5,3},{6,4},{7,5},{8,6},{9,7},{10,... | collective-permute-start | bytes 2312 | tf_op jit(solution)/shard_map/ppermute | solution.py:12
  83.3 3.0 %collective-permute-start.5 = (f32[192,1]{0,1:T(1,128)S(1)}, f32[192,1]{0,1:T(1,128)S(1)}, u32[]{:S(2)}, u32[]{:S(2)}) collective-permute-start(f32[192,1]{0,1:T(1,128)S(1)} %bitcast.51), channel_id=1, source_target_pairs={{0,13},{1,14},{2,15},{3,0},{4,1},{5,2},{6,3},{7,4},{8,5},{9,6},{10... | collective-permute-start | bytes 2312 | tf_op jit(solution)/shard_map/ppermute | solution.py:12
where the time goes:
time: 88.1 us; the launch traced here: 86.9 us
  waiting for transfers between devices  46.1 us (52%)
  matrix products  25.7 us (29%)
  local copies, waits for them, and re-layouts  8.26 us (9%)
  starting transfers between devices  5.24 us (6%)
  other arithmetic  0.93 us (1%)
    ppermute x6, waiting for transfers between devices, from_behind(): return lax.ppermute(value, axis, pairs)  46.1 us
    dot_general x4, matrix products, score_block(): lax.dot_general(train_grads, block, (((1,), (1,)), ((), ())), preferred_e...  22.2 us
    unnamed x10, local copies, waits for them, and re-layouts  5.55 us
    ppermute x6, starting transfers between devices, from_behind(): return lax.ppermute(value, axis, pairs)  5.24 us
    convert_element_type x1, local copies, waits for them, and re-layouts, precondition(): return outer.reshape(count, modules * side * side).astype(jnp.bfloat16)  2.71 us
  transfers between devices with their start and end apart: 6, of which 3 were waited for; matrix products, arithmetic and copies ran while one was open for 29% of the time, Pallas kernels for 0%

commit v1 on v0

v1 whole, which is shorter than its diff:
```python
import functools
import math

import jax
import jax.numpy as jnp
from jax import lax
from jax.experimental import pallas as pl
from jax.experimental.pallas import tpu as pltpu
from jax.sharding import PartitionSpec as P

SHIFTS = 3
SLOTS = SHIFTS + 1
WIDTH = 256
AHEAD = 4
RELAY = 1
ROWS = 256

F32 = jnp.float32
BF16 = jnp.bfloat16


def kernel(
    count, train_hbm, query_ref, left_ref, right_ref, scores_ref, mass_ref,
    train, spread, right_blocks, blocks, sums, visiting, train_sem, send_sem, recv_sem, sums_send, sums_recv,
):
    me = lax.axis_index("example")
    chip = me // 2
    first_core = lax.rem(me, 2) == 0
    odd_chip = lax.rem(chip, 2) == 1
    chunks, _, width = blocks.shape
    qrows = query_ref.shape[0]
    side = left_ref.shape[1]
    rows = train.shape[0]
    per = width // side
    scale = 1.0 / math.sqrt(side * side)

    def at(steps):
        return {"example": lax.rem(me + steps + count, count)}

    def slot(chunk, index):
        return blocks.at[chunk, pl.ds(index * qrows, qrows), :]

    def copy(chunk, source, steps, target, sem):
        return pltpu.make_async_remote_copy(
            src_ref=slot(chunk, source),
            dst_ref=slot(chunk, target),
            send_sem=send_sem.at[chunk, sem],
            recv_sem=recv_sem.at[chunk, target],
            device_id=at(steps),
            device_id_type=pl.DeviceIdType.MESH,
        )

    load = pltpu.make_async_copy(train_hbm, train, train_sem)
    load.start()
    barrier = pltpu.get_barrier_semaphore()
    for steps in (-3, -2, -1, 1, 2, 3):
        pl.semaphore_signal(barrier, inc=1, device_id=at(steps), device_id_type=pl.DeviceIdType.MESH)

    right_blocks[...] = jnp.zeros_like(right_blocks)
    for i in range(per):
        right_blocks[i * side:(i + 1) * side, i * side:(i + 1) * side] = right_ref[0]
    row_c = lax.broadcasted_iota(jnp.int32, (side, width), 0)
    lane = lax.broadcasted_iota(jnp.int32, (side, width), 1)
    same_c = row_c == lax.rem(lane, side)

    def produce(chunk):
        pick = (row_c == lane // side + chunk * per).astype(F32).astype(BF16)
        wide = lax.dot_general(left_ref[0], pick, (((0,), (0,)), ((), ())), preferred_element_type=F32)
        for b in range(side):
            value = jnp.broadcast_to(wide[b:b + 1, :], (side, width))
            spread[b * side:(b + 1) * side, :] = jnp.where(same_c, value, 0.0).astype(BF16)
        inner = jnp.dot(query_ref[...], spread[...], preferred_element_type=F32).astype(BF16)
        outer = jnp.dot(inner, right_blocks[...], preferred_element_type=F32)
        blocks[chunk, 0:qrows, :] = outer.astype(BF16)

    def send(chunk):
        @pl.when(first_core)
        def _():
            copy(chunk, 0, 2, 2, 1).start()
            copy(chunk, 0, 1, 1, 0).start()

        @pl.when(jnp.logical_not(first_core))
        def _():
            copy(chunk, 0, 3, 3, 0).start()

            @pl.when(jnp.logical_not(odd_chip))
            def _():
                copy(chunk, 0, 1, 1, 1).start()

    def relay(chunk):
        @pl.when(first_core)
        def _():
            copy(chunk, 0, 3, 3, 0).wait_recv()

            @pl.when(odd_chip)
            def _():
                copy(chunk, 3, -2, 1, 4).start()

    def gather(chunk):
        @pl.when(first_core)
        def _():
            copy(chunk, 0, 2, 2, 1).wait_recv()
            copy(chunk, 2, 1, 3, 3).start()
            copy(chunk, 0, 1, 1, 0).wait_recv()
            copy(chunk, 1, 1, 2, 2).start()

        @pl.when(jnp.logical_not(first_core))
        def _():
            for index in range(1, SLOTS):
                copy(chunk, 0, 1, index, 0).wait_recv()

    def finish(chunk):
        @pl.when(first_core)
        def _():
            for sem in range(4):
                copy(chunk, 0, 1, 1, sem).wait_send()

            @pl.when(odd_chip)
            def _():
                copy(chunk, 0, 1, 1, 4).wait_send()

        @pl.when(jnp.logical_not(first_core))
        def _():
            copy(chunk, 0, 1, 1, 0).wait_send()

            @pl.when(jnp.logical_not(odd_chip))
            def _():
                copy(chunk, 0, 1, 1, 1).wait_send()

    def product(chunk, row):
        columns = pl.ds(pl.multiple_of(chunk * width, width), width)
        return lax.dot_general(
            train[row:row + ROWS, columns], blocks[chunk], (((1,), (1,)), ((), ())), preferred_element_type=F32
        )

    produce(0)
    pl.semaphore_wait(barrier, 6)
    send(0)

    @pl.loop(1, AHEAD)
    def _(chunk):
        produce(chunk)
        send(chunk)

    scores_ref[...] = jnp.zeros_like(scores_ref)
    load.wait()
    for chunk in range(RELAY):
        relay(chunk)

    @pl.loop(0, chunks - 1)
    def _(chunk):
        @pl.when(chunk + AHEAD < chunks)
        def _():
            produce(chunk + AHEAD)
            send(chunk + AHEAD)

        @pl.when(chunk + RELAY < chunks)
        def _():
            relay(chunk + RELAY)

        gather(chunk)
        for row in range(0, rows, ROWS):
            scores_ref[row:row + ROWS, :] += product(chunk, row)

    gather(chunks - 1)
    total = jnp.zeros((1, SLOTS * qrows), F32)
    for row in range(0, rows, ROWS):
        part = (scores_ref[row:row + ROWS, :] + product(chunks - 1, row)) * scale
        scores_ref[row:row + ROWS, :] = part
        total = total + jnp.sum(part * part, axis=0, keepdims=True)
    for index in range(SLOTS):
        sums[index] = jnp.broadcast_to(total[:, index * qrows:(index + 1) * qrows], sums.shape[1:])
    returns = [
        pltpu.make_async_remote_copy(
            src_ref=sums.at[index],
            dst_ref=visiting.at[index],
            send_sem=sums_send.at[index],
            recv_sem=sums_recv.at[index],
            device_id=at(-index),
            device_id_type=pl.DeviceIdType.MESH,
        )
        for index in range(1, SLOTS)
    ]
    for back in returns:
        back.start()

    @pl.loop(0, chunks)
    def _(chunk):
        finish(chunk)

    for back in returns:
        back.wait()
    mass = sums[0] + visiting[1] + visiting[2] + visiting[3]
    mass_ref[...] = jnp.transpose(mass)[:, 0:1] / F32(SLOTS * rows)


def local(count, train_grads, query_grads, left_inverse, right_inverse):
    rows, mdim = train_grads.shape
    qrows = query_grads.shape[0]
    chunks = mdim // WIDTH
    vmem = pl.BlockSpec(memory_space=pltpu.VMEM)
    return pl.pallas_call(
        functools.partial(kernel, count),
        out_shape=(
            jax.ShapeDtypeStruct((rows, SLOTS * qrows), F32),
            jax.ShapeDtypeStruct((qrows, 1), F32),
        ),
        in_specs=[pl.BlockSpec(memory_space=pl.ANY), vmem, vmem, vmem],
        out_specs=(vmem, vmem),
        scratch_shapes=[
            pltpu.VMEM((rows, mdim), BF16),
            pltpu.VMEM((mdim, WIDTH), BF16),
            pltpu.VMEM((WIDTH, WIDTH), BF16),
            pltpu.VMEM((chunks, SLOTS * qrows, WIDTH), BF16),
            pltpu.VMEM((SLOTS, 8, qrows), F32),
            pltpu.VMEM((SLOTS, 8, qrows), F32),
            pltpu.SemaphoreType.DMA,
            pltpu.SemaphoreType.DMA((chunks, 5)),
            pltpu.SemaphoreType.DMA((chunks, SLOTS)),
            pltpu.SemaphoreType.DMA((SLOTS,)),
            pltpu.SemaphoreType.DMA((SLOTS,)),
        ],
        compiler_params=pltpu.CompilerParams(
            collective_id=0, has_side_effects=True, vmem_limit_bytes=40 * 1024 * 1024
        ),
    )(train_grads, query_grads, left_inverse, right_inverse)


def solution(mesh):
    return jax.shard_map(
        functools.partial(local, mesh.shape["example"]),
        mesh=mesh,
        in_specs=(
            P(("group", "example"), None),
            P(("group", "example"), None),
            P("group", None, None),
            P("group", None, None),
        ),
        out_specs=(P(("group", "example"), None), P(("group", "example"), None)),
        check_vma=False,
    )
```

time: 88.1 us -> 58 us (0.66)
  Pallas kernels: 0 us -> 48.5 us
  waiting for transfers between devices: 46.1 us -> 0 us
  matrix products: 25.7 us -> 0 us
  starting transfers between devices: 5.24 us -> 0 us
  other arithmetic: 0.93 us -> 0 us
    pallas_call x0 -> x1, Pallas kernels: none -> 48.5 us  [local(): pl.pallas_call(functools.partial(kernel, count), out_shape=(jax.ShapeDtyp...]
    ppermute x6 -> x0, waiting for transfers between devices: 46.1 us -> none  [from_behind(): return lax.ppermute(value, axis, pairs)]
    dot_general x6 -> x0, matrix products: 25.7 us -> none  [the longest x4 22.2 us: score_block(): lax.dot_general(train_grads, block, (((1,), (1,)), ((), ())), preferred_e...]
    ppermute x6 -> x0, starting transfers between devices: 5.24 us -> none  [from_behind(): return lax.ppermute(value, axis, pairs)]
    convert_element_type x1 -> x0, local copies, waits for them, and re-layouts: 2.71 us -> none  [precondition(): return outer.reshape(count, modules * side * side).astype(jnp.bfloat16)]
    unnamed x10 -> x9, local copies, waits for them, and re-layouts: 5.55 us -> 7.88 us
  transfers between devices with their start and end apart: 6 -> 0, of which waited for: 3 -> 0; matrix products, arithmetic and copies ran while one was open for 29% -> 0% of each run, Pallas kernels for 0% -> 0%
where the time goes in v1:
time: 58 us; the launch traced here: 57.6 us
  Pallas kernels  48.5 us (84%)
  local copies, waits for them, and re-layouts  8.52 us (15%)
  between operations  0.65 us (1%)
    pallas_call x1, Pallas kernels, local(): pl.pallas_call(functools.partial(kernel, count), out_shape=(jax.ShapeDtyp...  48.5 us
    unnamed x9, local copies, waits for them, and re-layouts  7.88 us

profile of v1, /device:TPU:0, one launch (start us, length us, event | category | flops | bytes accessed | tf_op | source)
XLA Modules:
  0.0 57.6 jit_solution(16751526388358079248)
XLA Ops:
  0.6 0.0 copy-start
  0.6 3.4 %copy-done = bf16[1024,4096]{1,0:T(8,128)(2,1)S(1)} copy-done((bf16[1024,4096]{1,0:T(8,128)(2,1)S(1)}, bf16[1024,4096]{1,0:T(8,128)(2,1)}, u32[]{:S(2)}) %copy-start) | copy-done | bytes 8388632
  4.0 0.0 copy-start.1
  4.0 1.4 %copy-done.1 = bf16[192,4096]{1,0:T(8,128)(2,1)S(1)} copy-done((bf16[192,4096]{1,0:T(8,128)(2,1)S(1)}, bf16[192,4096]{1,0:T(8,128)(2,1)}, u32[]{:S(2)}) %copy-start.1) | copy-done | bytes 1572888
  5.4 0.0 copy-start.2
  5.4 0.7 %copy-done.2 = bf16[1,64,64]{2,1,0:T(8,128)(2,1)S(1)} copy-done((bf16[1,64,64]{2,1,0:T(8,128)(2,1)S(1)}, bf16[1,64,64]{2,1,0:T(8,128)(2,1)}, u32[]{:S(2)}) %copy-start.2) | copy-done | bytes 8216
  6.1 0.0 copy-start.3
  6.1 0.7 %copy-done.3 = bf16[1,64,64]{2,1,0:T(8,128)(2,1)S(1)} copy-done((bf16[1,64,64]{2,1,0:T(8,128)(2,1)S(1)}, bf16[1,64,64]{2,1,0:T(8,128)(2,1)}, u32[]{:S(2)}) %copy-start.3) | copy-done | bytes 8216
  6.9 48.5 %shard_map.59 = (f32[1024,768]{1,0:T(8,128)S(1)}, f32[192,1]{1,0:T(8,128)S(1)}) custom-call(bf16[1024,4096]{1,0:T(8,128)(2,1)S(1)} %copy-done, bf16[192,4096]{1,0:T(8,128)(2,1)S(1)} %copy-done.1, bf16[1,64,64]{2,1,0:T(8,128)(2,1)S(1)} %copy-done.2, bf16[1,64,64]{2,1,0:T(8,128)(2,1)S(1)} %copy-done.3), custom_call_target="tpu_custom_call" | custom-call | tf_op jit(solution)/shard_map/pallas_call | solution.py:202
  55.3 0.6 %copy.6 = f32[192,1]{0,1:T(1,128)} copy(f32[192,1]{1,0:T(8,128)S(1)} %get-tuple-element.3) | data formatting | bytes 1536 | tf_op jit(solution)/shard_map/pallas_call | solution.py:202
  56.0 1.7 %copy.8 = f32[1024,768]{1,0:T(8,128)} copy(f32[1024,768]{1,0:T(8,128)S(1)} %get-tuple-element.6) | data formatting | bytes 6291456
Async XLA Ops:
  0.6 3.4 %copy-start = (bf16[1024,4096]{1,0:T(8,128)(2,1)S(1)}, bf16[1024,4096]{1,0:T(8,128)(2,1)}, u32[]{:S(2)}) copy-start(bf16[1024,4096]{1,0:T(8,128)(2,1)} %train_hbm.1) | copy-start | bytes 25165828
  4.0 1.4 %copy-start.1 = (bf16[192,4096]{1,0:T(8,128)(2,1)S(1)}, bf16[192,4096]{1,0:T(8,128)(2,1)}, u32[]{:S(2)}) copy-start(bf16[192,4096]{1,0:T(8,128)(2,1)} %query_ref.1) | copy-start | bytes 4718596
  5.4 0.7 %copy-start.2 = (bf16[1,64,64]{2,1,0:T(8,128)(2,1)S(1)}, bf16[1,64,64]{2,1,0:T(8,128)(2,1)}, u32[]{:S(2)}) copy-start(bf16[1,64,64]{2,1,0:T(8,128)(2,1)} %left_ref.1) | copy-start | bytes 24580
  6.1 0.7 %copy-start.3 = (bf16[1,64,64]{2,1,0:T(8,128)(2,1)S(1)}, bf16[1,64,64]{2,1,0:T(8,128)(2,1)}, u32[]{:S(2)}) copy-start(bf16[1,64,64]{2,1,0:T(8,128)(2,1)} %right_ref.1) | copy-start | bytes 24580

commit v2 on v1

v2 whole, which is shorter than its diff:
```python
import functools
import math

import jax
import jax.numpy as jnp
from jax import lax
from jax.experimental import pallas as pl
from jax.experimental.pallas import tpu as pltpu
from jax.sharding import PartitionSpec as P

SHIFTS = 3
SLOTS = SHIFTS + 1
WIDTH = 256
PIECES = 1
AHEAD = 4
VMEM_KIB = 58000
ROWS = 256

F32 = jnp.float32
BF16 = jnp.bfloat16


def kernel(
    count, train_hbm, query_hbm, left_hbm, right_hbm, scores_ref, mass_ref,
    train, query_ref, left_ref, right_ref, spread, right_blocks, blocks, sums, visiting, load_sem, send_sem, recv_sem, sums_send, sums_recv,
):
    me = lax.axis_index("example")
    chip = me // 2
    first_core = lax.rem(me, 2) == 0
    odd_chip = lax.rem(chip, 2) == 1
    chunks, _, width = blocks.shape
    qrows = query_ref.shape[0]
    prows = qrows // PIECES
    side = left_ref.shape[1]
    rows = train.shape[0]
    per = width // side
    scale = 1.0 / math.sqrt(side * side)

    def at(steps):
        return {"example": lax.rem(me + steps + count, count)}

    def slot(chunk, piece, index):
        return blocks.at[chunk, pl.ds(index * qrows + piece * prows, prows), :]

    def copy(chunk, piece, source, steps, target, sem):
        unit = chunk * PIECES + piece
        return pltpu.make_async_remote_copy(
            src_ref=slot(chunk, piece, source),
            dst_ref=slot(chunk, piece, target),
            send_sem=send_sem.at[unit, sem],
            recv_sem=recv_sem.at[unit, target],
            device_id=at(steps),
            device_id_type=pl.DeviceIdType.MESH,
        )

    barrier = pltpu.get_barrier_semaphore()
    for steps in (-3, -2, -1, 1, 2, 3):
        pl.semaphore_signal(barrier, inc=1, device_id=at(steps), device_id_type=pl.DeviceIdType.MESH)
    loads = [
        pltpu.make_async_copy(source, target, load_sem.at[index])
        for index, (source, target) in enumerate(
            ((left_hbm, left_ref), (right_hbm, right_ref), (query_hbm, query_ref), (train_hbm, train))
        )
    ]
    for load in loads:
        load.start()

    row_c = lax.broadcasted_iota(jnp.int32, (side, width), 0)
    lane = lax.broadcasted_iota(jnp.int32, (side, width), 1)
    same_c = row_c == lax.rem(lane, side)

    def build(chunk):
        pick = (row_c == lane // side + chunk * per).astype(F32).astype(BF16)
        wide = lax.dot_general(left_ref[0], pick, (((0,), (0,)), ((), ())), preferred_element_type=F32)
        for b in range(side):
            value = jnp.broadcast_to(wide[b:b + 1, :], (side, width))
            spread[b * side:(b + 1) * side, :] = jnp.where(same_c, value, 0.0).astype(BF16)

    def apply(chunk):
        inner = jnp.dot(query_ref[...], spread[...], preferred_element_type=F32).astype(BF16)
        outer = jnp.dot(inner, right_blocks[...], preferred_element_type=F32)
        blocks[chunk, 0:qrows, :] = outer.astype(BF16)

    def send(chunk):
        @pl.when(first_core)
        def _():
            for piece in range(PIECES):
                copy(chunk, piece, 0, 2, 2, 1).start()
                copy(chunk, piece, 0, 1, 1, 0).start()

        @pl.when(jnp.logical_not(first_core))
        def _():
            for piece in range(PIECES):
                copy(chunk, piece, 0, 3, 3, 0).start()

                @pl.when(jnp.logical_not(odd_chip))
                def _():
                    copy(chunk, piece, 0, 1, 1, 1).start()

    def relay(chunk):
        @pl.when(first_core)
        def _():
            for piece in range(PIECES):
                copy(chunk, piece, 0, 3, 3, 0).wait_recv()

                @pl.when(odd_chip)
                def _():
                    copy(chunk, piece, 3, -2, 1, 4).start()

    def gather(chunk):
        @pl.when(first_core)
        def _():
            for piece in range(PIECES):
                copy(chunk, piece, 0, 2, 2, 1).wait_recv()
                copy(chunk, piece, 2, 1, 3, 3).start()
                copy(chunk, piece, 0, 1, 1, 0).wait_recv()
                copy(chunk, piece, 1, 1, 2, 2).start()

        gather_near(chunk)

    def gather_near(chunk):
        @pl.when(jnp.logical_not(first_core))
        def _():
            for piece in range(PIECES):
                copy(chunk, piece, 0, 1, 1, 0).wait_recv()

    def gather_far(chunk):
        @pl.when(jnp.logical_not(first_core))
        def _():
            for piece in range(PIECES):
                for index in range(2, SLOTS):
                    copy(chunk, piece, 0, 1, index, 0).wait_recv()

    def finish(chunk):
        for piece in range(PIECES):
            @pl.when(first_core)
            def _():
                for sem in range(4):
                    copy(chunk, piece, 0, 1, 1, sem).wait_send()

                @pl.when(odd_chip)
                def _():
                    copy(chunk, piece, 0, 1, 1, 4).wait_send()

            @pl.when(jnp.logical_not(first_core))
            def _():
                copy(chunk, piece, 0, 1, 1, 0).wait_send()

                @pl.when(jnp.logical_not(odd_chip))
                def _():
                    copy(chunk, piece, 0, 1, 1, 1).wait_send()

    def product(chunk, row, first, last):
        columns = pl.ds(pl.multiple_of(chunk * width, width), width)
        return lax.dot_general(
            train[row:row + ROWS, columns], blocks[chunk, first:last, :], (((1,), (1,)), ((), ())),
            preferred_element_type=F32,
        )

    loads[0].wait()
    build(0)
    right_blocks[...] = jnp.zeros_like(right_blocks)
    for load in loads[1:3]:
        load.wait()
    for i in range(per):
        right_blocks[i * side:(i + 1) * side, i * side:(i + 1) * side] = right_ref[0]
    apply(0)
    pl.semaphore_wait(barrier, 6)
    send(0)

    @pl.loop(1, AHEAD)
    def _(chunk):
        build(chunk)
        apply(chunk)
        send(chunk)

    scores_ref[...] = jnp.zeros_like(scores_ref)
    loads[3].wait()
    relay(0)
    every = SLOTS * qrows

    @pl.loop(0, chunks // 2 - 1)
    def _(pair):
        chunk = pair * 2

        @pl.when(chunk + AHEAD < chunks)
        def _():
            for later in (chunk + AHEAD, chunk + AHEAD + 1):
                build(later)
                apply(later)
                send(later)

        for now in (chunk, chunk + 1):
            relay(now + 1)
            gather(now)
            gather_far(now)
        for row in range(0, rows, ROWS):
            scores_ref[row:row + ROWS, :] += product(chunk, row, 0, every) + product(chunk + 1, row, 0, every)

    relay(chunks - 1)
    gather(chunks - 2)
    gather_far(chunks - 2)
    for row in range(0, rows, ROWS):
        scores_ref[row:row + ROWS, :] += product(chunks - 2, row, 0, every)

    def last(first, end):
        total = jnp.zeros((1, end - first), F32)
        for row in range(0, rows, ROWS):
            part = (scores_ref[row:row + ROWS, first:end] + product(chunks - 1, row, first, end)) * scale
            scores_ref[row:row + ROWS, first:end] = part
            total = total + jnp.sum(part * part, axis=0, keepdims=True)
        return total

    gather(chunks - 1)
    near = last(0, every // 2)
    gather_far(chunks - 1)
    total = jnp.concatenate([near, last(every // 2, every)], axis=1)
    for index in range(SLOTS):
        sums[index] = jnp.broadcast_to(total[:, index * qrows:(index + 1) * qrows], sums.shape[1:])
    returns = [
        pltpu.make_async_remote_copy(
            src_ref=sums.at[index],
            dst_ref=visiting.at[index],
            send_sem=sums_send.at[index],
            recv_sem=sums_recv.at[index],
            device_id=at(-index),
            device_id_type=pl.DeviceIdType.MESH,
        )
        for index in range(1, SLOTS)
    ]
    for back in returns:
        back.start()

    @pl.loop(0, chunks)
    def _(chunk):
        finish(chunk)

    for back in returns:
        back.wait()
    mass = sums[0] + visiting[1] + visiting[2] + visiting[3]
    mass_ref[...] = mass[0:1, :] / F32(SLOTS * rows)


def local(count, train_grads, query_grads, left_inverse, right_inverse):
    rows, mdim = train_grads.shape
    qrows = query_grads.shape[0]
    chunks = mdim // WIDTH
    vmem = pl.BlockSpec(memory_space=pltpu.VMEM)
    scores, mass = pl.pallas_call(
        functools.partial(kernel, count),
        out_shape=(
            pltpu.VMEM((rows, SLOTS * qrows), F32),
            jax.ShapeDtypeStruct((1, qrows), F32),
        ),
        in_specs=[pl.BlockSpec(memory_space=pl.ANY)] * 4,
        out_specs=(vmem, vmem),
        scratch_shapes=[
            pltpu.VMEM((rows, mdim), BF16),
            pltpu.VMEM((qrows, mdim), BF16),
            pltpu.VMEM(left_inverse.shape, BF16),
            pltpu.VMEM(right_inverse.shape, BF16),
            pltpu.VMEM((mdim, WIDTH), BF16),
            pltpu.VMEM((WIDTH, WIDTH), BF16),
            pltpu.VMEM((chunks, SLOTS * qrows, WIDTH), BF16),
            pltpu.VMEM((SLOTS, 8, qrows), F32),
            pltpu.VMEM((SLOTS, 8, qrows), F32),
            pltpu.SemaphoreType.DMA((4,)),
            pltpu.SemaphoreType.DMA((chunks * PIECES, 5)),
            pltpu.SemaphoreType.DMA((chunks * PIECES, SLOTS)),
            pltpu.SemaphoreType.DMA((SLOTS,)),
            pltpu.SemaphoreType.DMA((SLOTS,)),
        ],
        compiler_params=pltpu.CompilerParams(
            collective_id=0, has_side_effects=True, vmem_limit_bytes=VMEM_KIB * 1024
        ),
    )(train_grads, query_grads, left_inverse, right_inverse)
    return scores, mass.reshape(qrows, 1)


def solution(mesh):
    return jax.shard_map(
        functools.partial(local, mesh.shape["example"]),
        mesh=mesh,
        in_specs=(
            P(("group", "example"), None),
            P(("group", "example"), None),
            P("group", None, None),
            P("group", None, None),
        ),
        out_specs=(P(("group", "example"), None), P(("group", "example"), None)),
        check_vma=False,
    )
```

time: 58 us -> 53.5 us (0.922)
  local copies, waits for them, and re-layouts: 8.52 us -> 2.23 us
  Pallas kernels: 48.5 us -> 50.4 us
    unnamed x9 -> x4, local copies, waits for them, and re-layouts: 7.88 us -> 2.23 us
    pallas_call x1, Pallas kernels: 48.5 us -> 50.4 us  [local(): pl.pallas_call(functools.partial(kernel, count), out_shape=(pltpu.VMEM((r...]
    pallas_call x1 -> x0, local copies, waits for them, and re-layouts: 0.64 us -> none  [local(): pl.pallas_call(functools.partial(kernel, count), out_shape=(jax.ShapeDtyp...]
where the time goes in v2:
time: 53.5 us; the launch traced here: 53.2 us
  Pallas kernels  50.4 us (94%)
  local copies, waits for them, and re-layouts  2.23 us (4%)
  between operations  0.65 us (1%)
    pallas_call x1, Pallas kernels, local(): pl.pallas_call(functools.partial(kernel, count), out_shape=(pltpu.VMEM((r...  50.4 us
    unnamed x4, local copies, waits for them, and re-layouts  2.23 us

profile of v2, /device:TPU:0, one launch (start us, length us, event | category | flops | bytes accessed | tf_op | source)
XLA Modules:
  0.0 53.2 jit_solution(15709577157772129453)
XLA Ops:
  0.6 50.4 %shard_map.59 = (f32[1024,768]{1,0:T(8,128)S(1)}, f32[1,192]{1,0:T(1,128)}) custom-call(bf16[1024,4096]{1,0:T(8,128)(2,1)} %train_hbm.1, bf16[192,4096]{1,0:T(8,128)(2,1)} %query_hbm.1, bf16[1,64,64]{2,1,0:T(8,128)(2,1)} %left_hbm.1, bf16[1,64,64]{2,1,0:T(8,128)(2,1)} %right_hbm.1), custom_call_target="tpu_custom_call" | custom-call | tf_op jit(solution)/shard_map/pallas_call | solution.py:249
  51.0 0.0 copy-start
  51.0 1.7 %copy.8 = f32[1024,768]{1,0:T(8,128)} copy(f32[1024,768]{1,0:T(8,128)S(1)} %get-tuple-element.6) | data formatting | bytes 6291456
  52.7 0.0 copy-done
  52.7 0.6 %copy.9 = f32[192,1]{0,1:T(1,128)} copy(f32[192,1]{0,1:T(1,128)S(1)} %bitcast.1) | data formatting | bytes 1536
Async XLA Ops:
  51.0 1.7 %copy-start = (f32[1,192]{1,0:T(1,128)S(1)}, f32[1,192]{1,0:T(1,128)}, u32[]{:S(2)}) copy-start(f32[1,192]{1,0:T(1,128)} %get-tuple-element.5) | copy-start | bytes 2308

commit v3 on v2

--- a/solution.py
+++ b/solution.py
@@ -183,19 +183,18 @@
     def _(pair):
         chunk = pair * 2
 
-        @pl.when(chunk + AHEAD < chunks)
-        def _():
-            for later in (chunk + AHEAD, chunk + AHEAD + 1):
-                build(later)
-                apply(later)
-                send(later)
-
         for now in (chunk, chunk + 1):
+            @pl.when(now + AHEAD < chunks)
+            def _():
+                build(now + AHEAD)
+                apply(now + AHEAD)
+                send(now + AHEAD)
+
             relay(now + 1)
             gather(now)
             gather_far(now)
-        for row in range(0, rows, ROWS):
-            scores_ref[row:row + ROWS, :] += product(chunk, row, 0, every) + product(chunk + 1, row, 0, every)
+            for row in range(0, rows, ROWS):
+                scores_ref[row:row + ROWS, :] += product(now, row, 0, every)
 
     relay(chunks - 1)
     gather(chunks - 2)

time: 53.5 us -> 52.6 us (0.983)
  Pallas kernels: 50.4 us -> 49.5 us
    pallas_call x1, Pallas kernels: 50.4 us -> 49.5 us  [local(): pl.pallas_call(functools.partial(kernel, count), out_shape=(pltpu.VMEM((r...]
where the time goes in v3:
time: 52.6 us; the launch traced here: 52.4 us
  Pallas kernels  49.5 us (94%)
  local copies, waits for them, and re-layouts  2.23 us (4%)
  between operations  0.65 us (1%)
    pallas_call x1, Pallas kernels, local(): pl.pallas_call(functools.partial(kernel, count), out_shape=(pltpu.VMEM((r...  49.5 us
    unnamed x4, local copies, waits for them, and re-layouts  2.23 us

profile of v3, /device:TPU:0, one launch (start us, length us, event | category | flops | bytes accessed | tf_op | source)
XLA Modules:
  0.0 52.4 jit_solution(14768111255748146705)
XLA Ops:
  0.6 49.5 %shard_map.59 = (f32[1024,768]{1,0:T(8,128)S(1)}, f32[1,192]{1,0:T(1,128)}) custom-call(bf16[1024,4096]{1,0:T(8,128)(2,1)} %train_hbm.1, bf16[192,4096]{1,0:T(8,128)(2,1)} %query_hbm.1, bf16[1,64,64]{2,1,0:T(8,128)(2,1)} %left_hbm.1, bf16[1,64,64]{2,1,0:T(8,128)(2,1)} %right_hbm.1), custom_call_target="tpu_custom_call" | custom-call | tf_op jit(solution)/shard_map/pallas_call | solution.py:248
  50.2 0.0 copy-start
  50.2 1.7 %copy.8 = f32[1024,768]{1,0:T(8,128)} copy(f32[1024,768]{1,0:T(8,128)S(1)} %get-tuple-element.6) | data formatting | bytes 6291456
  51.8 0.0 copy-done
  51.8 0.6 %copy.9 = f32[192,1]{0,1:T(1,128)} copy(f32[192,1]{0,1:T(1,128)S(1)} %bitcast.1) | data formatting | bytes 1536
Async XLA Ops:
  50.2 1.7 %copy-start = (f32[1,192]{1,0:T(1,128)S(1)}, f32[1,192]{1,0:T(1,128)}, u32[]{:S(2)}) copy-start(f32[1,192]{1,0:T(1,128)} %get-tuple-element.5) | copy-start | bytes 2308
